TPU v7x, 32 devices: a whole 2x2x4 slice. The times are simulated.
32 devices in a mesh: dp: 8 (over y, x, core), pipe: 4 (over z).
Axes of the slice: x: 2, y: 2, z: 4, core: 2. Of those that a mesh axis runs over, the one named last changes fastest.
Arguments:
- queries: bfloat16 [4, 1920, 2560], P('pipe', 'dp'), may hold values from -6 to 6
- key_rows: bfloat16 [4, 1920, 512], P('pipe', 'dp'), may hold values from -6 to 6
- value_rows: bfloat16 [4, 1920, 512], P('pipe', 'dp'), may hold values from -6 to 6
- out_grad: bfloat16 [4, 1920, 2560], P('pipe', 'dp'), may hold values from -6 to 6
- log_norm: bfloat16 [4, 20, 1920], P('pipe', None, 'dp'), may hold values from 2.5 to 4.5
- row_delta: bfloat16 [4, 20, 1920], P('pipe', None, 'dp'), may hold values from -24 to 24
- cand_lengths: int32 [4, 8, 3], P('pipe', 'dp'), may hold values from 0 to 80, as said below
Outputs:
- up_q: bfloat16 [4, 1920, 2560], P('pipe', 'dp')
- up_k: bfloat16 [4, 1920, 512], P('pipe', 'dp')
- up_v: bfloat16 [4, 1920, 512], P('pipe', 'dp')
- bias_grad: float32 [4, 3072], P('pipe', 'dp')
- value_bias_grad: float32 [4, 512], P('pipe', 'dp')
Inputs may be any that keep to these rules, and one draw needn't show every extreme that they name: `cand_lengths`: each block's candidates fill its slots from the front, zeros marking empty slots, and the first slot is never empty; nonzero lengths are 64 or more, and the lengths of one block sum to at most 240. For the blocks i and i + 4 of one section, the rows of one block's candidates that end within its first 160 rows plus the rows of the other block's candidates that end beyond them come to at most 160, both ways round.
All inputs are finite; a program needn't handle non-finite values.
Results may differ from a plain program's by a relative error of at most 0.0054.
Values may be sent and summed in bfloat16 or wider, within the bound.
A program may use at most 64 MiB of HBM per device.

v0:
```python
import math

import jax
import jax.numpy as jnp
from jax import lax
from jax.sharding import PartitionSpec as P

HEADS = 20
KV_HEADS = 4
HEAD_DIM = 128
HOME_ROWS = 240


def passed_along(value, axis, steps):
    count = lax.axis_size(axis)
    pairs = [(source, (source + steps) % count) for source in range(count)]
    return lax.ppermute(value, axis, pairs)


def segment_mask(lengths, row_count):
    row_ends = jnp.cumsum(lengths)
    position = jnp.arange(row_count, dtype=jnp.int32)
    labels = jnp.sum((position[:, None] >= row_ends[None, :]).astype(jnp.int32), axis=1)
    inside = position < row_ends[-1]
    return (labels[:, None] == labels[None, :]) & inside[:, None] & inside[None, :]


def attend_backward(query_rows, key_part, value_part, grad_rows, norm_rows, delta_rows, allowed):
    row_count = query_rows.shape[0]
    per_group = HEADS // KV_HEADS
    factor = 1.0 / math.sqrt(HEAD_DIM)
    query_groups = jnp.moveaxis(query_rows.reshape(row_count, KV_HEADS, per_group * HEAD_DIM), 1, 0)
    grad_groups = jnp.moveaxis(grad_rows.reshape(row_count, KV_HEADS, per_group * HEAD_DIM), 1, 0)
    key_groups = jnp.moveaxis(key_part.reshape(row_count, KV_HEADS, HEAD_DIM), 1, 0)
    value_groups = jnp.moveaxis(value_part.reshape(row_count, KV_HEADS, HEAD_DIM), 1, 0)
    norm_groups = norm_rows.reshape(KV_HEADS, per_group, row_count)
    delta_groups = delta_rows.reshape(KV_HEADS, per_group, row_count)

    def one_group(pieces):
        query_part, key_group, value_group, grad_part, norm_part, delta_part = pieces
        query_heads = query_part.reshape(row_count, per_group, HEAD_DIM)
        grad_heads = grad_part.reshape(row_count, per_group, HEAD_DIM)
        scores = (
            jnp.einsum("igd,jd->gij", query_heads, key_group, preferred_element_type=jnp.float32)
            * factor
        )
        shifted = scores - norm_part.astype(jnp.float32)[:, :, None]
        probs = jnp.where(allowed[None], jnp.exp(shifted), 0.0)
        dprobs = jnp.einsum(
            "igd,jd->gij", grad_heads, value_group, preferred_element_type=jnp.float32
        )
        dscores = probs * (dprobs - delta_part.astype(jnp.float32)[:, :, None])
        probs_low = probs.astype(jnp.bfloat16)
        dscores_low = dscores.astype(jnp.bfloat16)
        grad_value = jnp.einsum(
            "gij,igd->jd", probs_low, grad_heads, preferred_element_type=jnp.float32
        )
        grad_key = (
            jnp.einsum("gij,igd->jd", dscores_low, query_heads, preferred_element_type=jnp.float32)
            * factor
        )
        grad_query = (
            jnp.einsum("gij,jd->igd", dscores_low, key_group, preferred_element_type=jnp.float32)
            * factor
        )
        return (
            grad_query.reshape(row_count, per_group * HEAD_DIM).astype(jnp.bfloat16),
            grad_key.astype(jnp.bfloat16),
            grad_value.astype(jnp.bfloat16),
        )

    grad_query, grad_key, grad_value = lax.map(
        one_group, (query_groups, key_groups, value_groups, grad_groups, norm_groups, delta_groups)
    )
    grad_query = jnp.moveaxis(grad_query, 0, 1).reshape(row_count, HEADS * HEAD_DIM)
    grad_key = jnp.moveaxis(grad_key, 0, 1).reshape(row_count, KV_HEADS * HEAD_DIM)
    grad_value = jnp.moveaxis(grad_value, 0, 1).reshape(row_count, KV_HEADS * HEAD_DIM)
    return (grad_query, grad_key, grad_value)


def send_up(gradients):
    return passed_along((gradients[0], gradients[1], gradients[2]), "pipe", -1)


def column_totals(parts):
    ones_row = jnp.ones((1, HOME_ROWS), jnp.bfloat16)
    query_key = jnp.concatenate(
        [
            jnp.dot(ones_row, parts[0], preferred_element_type=jnp.float32)[0],
            jnp.dot(ones_row, parts[1], preferred_element_type=jnp.float32)[0],
        ]
    )
    value_part = jnp.dot(ones_row, parts[2], preferred_element_type=jnp.float32)[0]
    return (query_key, value_part)


def shards(queries, key_rows, value_rows, out_grad, log_norm, row_delta, cand_lengths):
    query_home = queries[0]
    key_home = key_rows[0]
    value_home = value_rows[0]
    grad_home = out_grad[0]
    norm_home = log_norm[0]
    delta_home = row_delta[0]
    lengths = cand_lengths[0, 0]
    allowed = segment_mask(lengths, HOME_ROWS)
    gradients = attend_backward(
        query_home, key_home, value_home, grad_home, norm_home, delta_home, allowed
    )
    received = send_up(gradients)
    query_key_sums, value_sums = column_totals(received)
    bias_grad, value_bias_grad = (
        lax.psum_scatter(query_key_sums, "dp", scatter_dimension=0, tiled=True),
        lax.psum_scatter(value_sums, "dp", scatter_dimension=0, tiled=True),
    )
    return (
        received[0][None],
        received[1][None],
        received[2][None],
        bias_grad[None],
        value_bias_grad[None],
    )


def solution(mesh):
    in_specs = (
        P("pipe", "dp", None),
        P("pipe", "dp", None),
        P("pipe", "dp", None),
        P("pipe", "dp", None),
        P("pipe", None, "dp"),
        P("pipe", None, "dp"),
        P("pipe", "dp", None),
    )
    out_specs = (
        P("pipe", "dp", None),
        P("pipe", "dp", None),
        P("pipe", "dp", None),
        P("pipe", "dp"),
        P("pipe", "dp"),
    )
    return jax.shard_map(shards, mesh=mesh, in_specs=in_specs, out_specs=out_specs, check_vma=False)
```

profile of v0, /device:TPU:0, one launch (start us, length us, event | category | flops | bytes accessed | tf_op | source)
XLA Modules:
  0.0 105.2 jit_solution(2330388597104448430)
XLA Ops:
  0.7 0.9 reduce-window.4
  2.9 0.7 reshape_squeeze.20
  4.4 1.0 reshape_squeeze.18
  5.5 0.7 copy.50
  6.6 1.4 %copy.49 = bf16[4,240,640]{1,2,0:T(8,128)(2,1)S(1)} copy(bf16[4,240,640]{2,0,1:T(4,128)(2,1)S(1)} %bitcast.148) | data formatting | bytes 2457600
  8.0 3.5 %reshape_squeeze.22 = bf16[240,4,640]{2,1,0:T(4,128)(2,1)} reshape(bf16[1,240,2560]{2,1,0:T(8,128)(2,1)} %param.12) | data formatting | bytes 2457600 | tf_op jit(solution)/shard_map/reshape;squeeze | solution.py:33
  11.4 2.6 %copy.51 = bf16[4,240,640]{1,2,0:T(8,128)(2,1)S(1)} copy(bf16[4,240,640]{2,0,1:T(4,128)(2,1)} %bitcast.149) | data formatting | bytes 2457600
  14.1 20.2 %while.15 = (s32[]{:T(128)}, bf16[4,240,640]{1,2,0:T(8,128)(2,1)}, bf16[4,240,128]{2,1,0:T(8,128)(2,1)}, bf16[4,240,128]{2,1,0:T(8,128)(2,1)}, bf16[4,240,128]{2...) while((s32[]{:T(128)}, bf16[4,240,640]{1,2,0:T(8,128)(2,1)}, ...), condition=%wide.region_3.4_spmd.clone, body=%wide.region_2.3_spmd.clone.sunk | while | flops 371230560 | bytes 9711957 | solution.py:72
  14.7 1.0 fusion.76
  15.7 1.1 %fusion.73 = bf16[5,240,240]{1,2,0:T(8,128)(2,1)S(1)} fusion(f32[5,240,240]{1,2,0:T(8,128)S(1)} %fusion.72, bf16[240,5,128]{0,2,1:T(8,128)(2,1)S(1)} %bitcast.143, f32[5,240]{1,0:T(8,128)S(1)} %get-tuple-element.241, bf16[4,240,128]{2,1,0:T(8,128)(2,1)} %get-tuple-element.275, s32[]{:T(128)S(6)} %copy.74), kind=kOutput, calls=%fused_computation.9.clone.1 | convolution fusion | flops 74592000 | bytes 2101444 | tf_op jit(solution)/shard_map/while/body/eval_jaxpr/igd,jd->gij/dot_general | solution.py:49
  16.8 1.0 fusion.75
  18.4 0.7 constant_dynamic-update-slice_fusion.2
  19.7 1.0 fusion.76
  20.7 1.1 %fusion.73 = bf16[5,240,240]{1,2,0:T(8,128)(2,1)S(1)} fusion(f32[5,240,240]{1,2,0:T(8,128)S(1)} %fusion.72, bf16[240,5,128]{0,2,1:T(8,128)(2,1)S(1)} %bitcast.143, f32[5,240]{1,0:T(8,128)S(1)} %get-tuple-element.241, bf16[4,240,128]{2,1,0:T(8,128)(2,1)} %get-tuple-element.275, s32[]{:T(128)S(6)} %copy.74), kind=kOutput, calls=%fused_computation.9.clone.1 | convolution fusion | flops 74592000 | bytes 2101444 | tf_op jit(solution)/shard_map/while/body/eval_jaxpr/igd,jd->gij/dot_general | solution.py:49
  21.8 1.0 fusion.75
  23.4 0.8 constant_dynamic-update-slice_fusion.2
  24.8 1.0 fusion.76
  25.7 1.1 %fusion.73 = bf16[5,240,240]{1,2,0:T(8,128)(2,1)S(1)} fusion(f32[5,240,240]{1,2,0:T(8,128)S(1)} %fusion.72, bf16[240,5,128]{0,2,1:T(8,128)(2,1)S(1)} %bitcast.143, f32[5,240]{1,0:T(8,128)S(1)} %get-tuple-element.241, bf16[4,240,128]{2,1,0:T(8,128)(2,1)} %get-tuple-element.275, s32[]{:T(128)S(6)} %copy.74), kind=kOutput, calls=%fused_computation.9.clone.1 | convolution fusion | flops 74592000 | bytes 2101444 | tf_op jit(solution)/shard_map/while/body/eval_jaxpr/igd,jd->gij/dot_general | solution.py:49
  26.9 1.0 fusion.75
  28.5 0.8 constant_dynamic-update-slice_fusion.2
  29.8 1.0 fusion.76
  30.8 1.1 %fusion.73 = bf16[5,240,240]{1,2,0:T(8,128)(2,1)S(1)} fusion(f32[5,240,240]{1,2,0:T(8,128)S(1)} %fusion.72, bf16[240,5,128]{0,2,1:T(8,128)(2,1)S(1)} %bitcast.143, f32[5,240]{1,0:T(8,128)S(1)} %get-tuple-element.241, bf16[4,240,128]{2,1,0:T(8,128)(2,1)} %get-tuple-element.275, s32[]{:T(128)S(6)} %copy.74), kind=kOutput, calls=%fused_computation.9.clone.1 | convolution fusion | flops 74592000 | bytes 2101444 | tf_op jit(solution)/shard_map/while/body/eval_jaxpr/igd,jd->gij/dot_general | solution.py:49
  31.9 1.0 fusion.75
  33.5 0.8 constant_dynamic-update-slice_fusion.2
  34.3 1.6 %copy.60 = bf16[240,2560]{1,0:T(8,128)(2,1)S(1)} copy(bf16[240,2560]{0,1:T(8,128)(2,1)} %bitcast.150) | data formatting | bytes 2457600 | tf_op jit(solution)/shard_map/reshape | solution.py:75
  35.9 5.1 %collective-permute-start = (bf16[240,2560]{1,0:T(8,128)(2,1)S(1)}, bf16[240,2560]{1,0:T(8,128)(2,1)S(1)}, u32[]{:S(2)}, u32[]{:S(2)}) collective-permute-start(bf16[240,2560]{1,0:T(8,128)(2,1)S(1)} %copy.60), channel_id=1, source_target_pairs={{0,3},{1,0},{2,1},{3,2},{4,7},{5,4},{6,5},{7,6},{8,11},{9,8},{10,9... | collective-permute-start | bytes 3686408 | tf_op jit(solution)/shard_map/ppermute | solution.py:17
  41.0 1.0 copy_bitcast_fusion.1
  42.5 1.0 copy_bitcast_fusion
  45.8 27.9 %collective-permute-done.1 = bf16[240,512]{1,0:T(8,128)(2,1)S(1)} collective-permute-done((bf16[240,512]{1,0:T(8,128)(2,1)S(1)}, bf16[240,512]{1,0:T(8,128)(2,1)S(1)}, u32[]{:S(2)}, u32[]{:S(2)}) %collective-permute-start.1) | collective-permute-done | bytes 245792 | tf_op jit(solution)/shard_map/ppermute | solution.py:17
  73.7 4.1 %collective-permute-done.2 = bf16[240,512]{1,0:T(8,128)(2,1)S(1)} collective-permute-done((bf16[240,512]{1,0:T(8,128)(2,1)S(1)}, bf16[240,512]{1,0:T(8,128)(2,1)S(1)}, u32[]{:S(2)}, u32[]{:S(2)}) %collective-permute-start.2) | collective-permute-done | bytes 245792 | tf_op jit(solution)/shard_map/ppermute | solution.py:17
  78.4 23.2 %all-reduce.2 = (f32[3072]{0:T(1024)S(1)}, f32[512]{0:T(512)S(1)}) all-reduce(f32[3072]{0:T(1024)S(1)} %pad_maximum_fusion, f32[512]{0:T(512)S(1)} %bitcast.155), channel_id=2, replica_groups=mesh['dp'=8,'pipe'=4] {'dp'}, use_global_device_ids=true, to_apply=%region_4.5.clone | all-reduce | flops 3584 | bytes 28672
  102.8 1.0 copy.87
  (53 shorter events, 12.0 us)
Async XLA Ops:
  0.6 4.8 %copy-start.1 = (bf16[1,240,512]{2,1,0:T(8,128)(2,1)S(1)}, bf16[1,240,512]{2,1,0:T(8,128)(2,1)}, u32[]{:S(2)}) copy-start(bf16[1,240,512]{2,1,0:T(8,128)(2,1)} %param.11) | copy-start | bytes 737284
  0.6 5.6 %copy-start = (bf16[1,240,2560]{2,1,0:T(8,128)(2,1)S(1)}, bf16[1,240,2560]{2,1,0:T(8,128)(2,1)}, u32[]{:S(2)}) copy-start(bf16[1,240,2560]{2,1,0:T(8,128)(2,1)} %param.9) | copy-start | bytes 3686404
  34.3 9.6 %copy-start.2 = (u32[32]{0:T(128)S(1)}, u32[32]{0:T(128)}, u32[]{:S(2)}) copy-start(u32[32]{0:T(128)} %constant.44) | copy-start | bytes 388
  35.9 42.2 %collective-permute-start = (bf16[240,2560]{1,0:T(8,128)(2,1)S(1)}, bf16[240,2560]{1,0:T(8,128)(2,1)S(1)}, u32[]{:S(2)}, u32[]{:S(2)}) collective-permute-start(bf16[240,2560]{1,0:T(8,128)(2,1)S(1)} %copy.60), channel_id=1, source_target_pairs={{0,3},{1,0},{2,1},{3,2},{4,7},{5,4},{6,5},{7,6},{8,11},{9,8},{10,9... | collective-permute-start | bytes 3686408 | tf_op jit(solution)/shard_map/ppermute | solution.py:17
  42.0 31.7 %collective-permute-start.1 = (bf16[240,512]{1,0:T(8,128)(2,1)S(1)}, bf16[240,512]{1,0:T(8,128)(2,1)S(1)}, u32[]{:S(2)}, u32[]{:S(2)}) collective-permute-start(bf16[240,512]{1,0:T(8,128)(2,1)S(1)} %copy_bitcast_fusion.1), channel_id=1, source_target_pairs={{0,3},{1,0},{2,1},{3,2},{4,7},{5,4},{6,5},{7,6},{8,11},{9,8},{10,9... | collective-permute-start | bytes 737288 | tf_op jit(solution)/shard_map/ppermute | solution.py:17
  43.4 34.4 %collective-permute-start.2 = (bf16[240,512]{1,0:T(8,128)(2,1)S(1)}, bf16[240,512]{1,0:T(8,128)(2,1)S(1)}, u32[]{:S(2)}, u32[]{:S(2)}) collective-permute-start(bf16[240,512]{1,0:T(8,128)(2,1)S(1)} %copy_bitcast_fusion), channel_id=1, source_target_pairs={{0,3},{1,0},{2,1},{3,2},{4,7},{5,4},{6,5},{7,6},{8,11},{9,8},{10,9... | collective-permute-start | bytes 737288 | tf_op jit(solution)/shard_map/ppermute | solution.py:17
where the time goes:
time: 106 us; the launch traced here: 105 us
  waiting for transfers between devices  32 us (30%)
  local copies, waits for them, and re-layouts  23.3 us (22%)
  blocking collectives  23.2 us (22%)
  matrix products  16.1 us (15%)
  starting transfers between devices  6.1 us (6%)
  other arithmetic  2.22 us (2%)
  between operations  2.06 us (2%)
    ppermute x3, waiting for transfers between devices, passed_along(): return lax.ppermute(value, axis, pairs)  32 us
    unnamed x1, blocking collectives  23.2 us
    unnamed x15, local copies, waits for them, and re-layouts  7.87 us
    ppermute x3, starting transfers between devices, passed_along(): return lax.ppermute(value, axis, pairs)  6.1 us
    dot_general x4, matrix products, one_group(): jnp.einsum('igd,jd->gij', grad_heads, value_group, preferred_element_type...  4.55 us
    dot_general x4, matrix products, one_group(): jnp.einsum('gij,igd->jd', dscores_low, query_heads, preferred_element_typ...  3.86 us
    dot_general x4, matrix products, one_group(): jnp.einsum('gij,igd->jd', probs_low, grad_heads, preferred_element_type=j...  3.85 us
    another operation x1, local copies, waits for them, and re-layouts, attend_backward(): grad_rows.reshape(row_count, KV_HEADS, per_group * HEAD_DIM)  3.45 us
  transfers between devices with their start and end apart: 3, of which 2 were waited for; matrix products, arithmetic and copies ran while one was open for 3% of the time, Pallas kernels for 0%

commit v1 on v0

v1 whole, which is shorter than its diff:
```python
import functools
import math

import jax
import jax.numpy as jnp
from jax import lax
from jax.experimental import pallas as pl
from jax.experimental.pallas import tpu as pltpu
from jax.sharding import PartitionSpec as P

HEADS = 20
KV_HEADS = 4
HEAD_DIM = 128
PER_GROUP = HEADS // KV_HEADS
QUERY_WIDTH = PER_GROUP * HEAD_DIM
CHUNK = QUERY_WIDTH + 2 * HEAD_DIM
SLOT = 80
SLOTS = 3
FACTOR = 1.0 / math.sqrt(HEAD_DIM)
MESH = pl.DeviceIdType.MESH


def up_to_lanes(width):
    return -(-width // 128) * 128


def dot(a, b, dims):
    return lax.dot_general(a, b, (dims, ((), ())), preferred_element_type=jnp.float32)


def placement(lengths, rows, transposed):
    shape = (SLOTS * SLOT, rows) if not transposed else (rows, SLOTS * SLOT)
    slot_row = lax.broadcasted_iota(jnp.int32, shape, 1 if transposed else 0)
    row = lax.broadcasted_iota(jnp.int32, shape, 0 if transposed else 1)
    found = jnp.zeros(shape, jnp.float32)
    begin = jnp.zeros_like(lengths[0])
    for c in range(SLOTS):
        inside = slot_row - c * SLOT
        hit = (inside >= 0) & (inside < lengths[c]) & (row == inside + begin)
        found = jnp.where(hit, 1.0, found)
        begin = begin + lengths[c]
    return found.astype(jnp.bfloat16)


def kernel(
    dp, pipe, lengths_ref, q_ref, k_ref, v_ref, g_ref, norm_ref, delta_ref,
    up_q_ref, up_k_ref, up_v_ref, bias_ref, value_bias_ref,
    home_out, side_out, own_second, pair_out, home_in, side_in, pair_in, back_in,
    length_out, length_in, sums, sums_in, piece_out, piece_in,
    home_sem, side_sem, pair_sem, back_sem, length_sem, sums_sem, piece_sem,
):
    me, stage = lax.axis_index("dp"), lax.axis_index("pipe")
    before = {"dp": me, "pipe": (stage + pipe - 1) % pipe}
    after = {"dp": me, "pipe": (stage + 1) % pipe}
    steps = [1 << i for i in range(dp.bit_length() - 1)]

    def across(step):
        return {"dp": me + step - 2 * step * ((me // step) % 2), "pipe": stage}

    pair = across(dp // 2)
    barrier = pltpu.get_barrier_semaphore()
    greeted = [before, after] + [across(step) for step in steps]
    for device in greeted:
        pl.semaphore_signal(barrier, inc=1, device_id=device, device_id_type=MESH)
    pl.semaphore_wait(barrier, len(greeted))

    def remote(src, dst, sem, device):
        return pltpu.make_async_remote_copy(
            src_ref=src, dst_ref=dst, send_sem=sem.at[0], recv_sem=sem.at[1],
            device_id=device, device_id_type=MESH,
        )

    lengths = [lengths_ref[0, 0, c] for c in range(SLOTS)]
    line = lax.broadcasted_iota(jnp.int32, (8, 128), 0)
    length_out[...] = jnp.where(
        line == 0, lengths[0], jnp.where(line == 1, lengths[1], lengths[2])
    )
    length_copy = remote(length_out, length_in, length_sem, before)
    length_copy.start()

    rows = q_ref.shape[0]
    gather = placement(lengths, rows, False)
    norm_cols = dot(gather, norm_ref[...], ((1,), (1,)))
    delta_cols = dot(gather, delta_ref[...], ((1,), (1,)))
    column = lax.broadcasted_iota(jnp.int32, (PER_GROUP * SLOT, SLOT), 1)
    ones = jnp.ones((8, SLOTS * SLOT), jnp.bfloat16)

    home = [remote(home_out.at[g], home_in.at[g], home_sem.at[g], before) for g in range(KV_HEADS)]
    side = [remote(side_out.at[g], side_in.at[g], side_sem.at[g], before) for g in range(KV_HEADS)]
    lend = [remote(pair_out.at[g], pair_in.at[g], pair_sem.at[g], pair) for g in range(KV_HEADS)]
    back = [remote(side_in.at[g], back_in.at[g], back_sem.at[g], pair) for g in range(KV_HEADS)]

    def taken(ref, begin, width):
        return dot(gather, ref[:, begin : begin + width], ((1,), (0,))).astype(jnp.bfloat16)

    def send_side(g):
        lend[g].wait_recv()
        side_out[g] = own_second[g] + pair_in[g]
        side[g].start()

    for g in range(KV_HEADS):
        queries = taken(q_ref, g * QUERY_WIDTH, QUERY_WIDTH)
        grads = taken(g_ref, g * QUERY_WIDTH, QUERY_WIDTH)
        keys = taken(k_ref, g * HEAD_DIM, HEAD_DIM)
        values = taken(v_ref, g * HEAD_DIM, HEAD_DIM)
        for c in (2, 0, 1):
            at = slice(c * SLOT, (c + 1) * SLOT)
            heads = range(PER_GROUP)

            def stacked(x):
                return jnp.concatenate(
                    [x[at, h * HEAD_DIM : (h + 1) * HEAD_DIM] for h in heads], axis=0
                )

            def per_row(x):
                return jnp.concatenate(
                    [x[at, g * PER_GROUP + h : g * PER_GROUP + h + 1] for h in heads], axis=0
                )

            query, grad, key, value = stacked(queries), stacked(grads), keys[at], values[at]
            scores = dot(query, key, ((1,), (1,))) * FACTOR
            probs = jnp.where(column < lengths[c], jnp.exp(scores - per_row(norm_cols)), 0.0)
            dprobs = dot(grad, value, ((1,), (1,)))
            dscores = (probs * (dprobs - per_row(delta_cols))).astype(jnp.bfloat16)
            probs = probs.astype(jnp.bfloat16)
            grad_v = dot(probs, grad, ((0,), (0,))).astype(jnp.bfloat16)
            grad_k = (dot(dscores, query, ((0,), (0,))) * FACTOR).astype(jnp.bfloat16)
            grad_q = (dot(dscores, key, ((1,), (0,))) * FACTOR).astype(jnp.bfloat16)
            held = (home_out, own_second, pair_out)[c]
            for h in heads:
                held[g, :, h * HEAD_DIM : (h + 1) * HEAD_DIM] = grad_q[h * SLOT : (h + 1) * SLOT]
            held[g, :, QUERY_WIDTH : QUERY_WIDTH + HEAD_DIM] = grad_k
            held[g, :, QUERY_WIDTH + HEAD_DIM :] = grad_v
            if c == 2:
                lend[g].start()
            if c == 0:
                home[g].start()
        total = dot(
            ones,
            jnp.concatenate([home_out[g], own_second[g], pair_out[g]], axis=0),
            ((1,), (0,)),
        )[:1]
        sums[0, :, g * QUERY_WIDTH : (g + 1) * QUERY_WIDTH] = total[:, :QUERY_WIDTH]
        for i in range(2):
            begin = HEADS * HEAD_DIM + (i * KV_HEADS + g) * HEAD_DIM
            part = QUERY_WIDTH + i * HEAD_DIM
            sums[0, :, begin : begin + HEAD_DIM] = total[:, part : part + HEAD_DIM]
        if g > 0:
            send_side(g - 1)
    send_side(KV_HEADS - 1)

    exchanges = []
    for i, step in enumerate(steps):
        exchange = remote(sums.at[i], sums_in.at[i], sums_sem.at[i], across(step))
        exchange.start()
        exchange.wait_recv()
        sums[i + 1] = sums[i] + sums_in[i]
        exchanges.append(exchange)
    total = sums[len(steps)]
    width, value_width = bias_ref.shape[1], value_bias_ref.shape[1]
    value_at = up_to_lanes(width)
    value_from = (HEADS + KV_HEADS) * HEAD_DIM
    bias = jnp.zeros((1, width), jnp.float32)
    value_bias = jnp.zeros((1, value_width), jnp.float32)
    for j in range(dp):
        bias = jnp.where(me == j, total[:, j * width : (j + 1) * width], bias)
        value_begin = value_from + j * value_width
        value_bias = jnp.where(me == j, total[:, value_begin : value_begin + value_width], value_bias)
    piece_out[...] = jnp.zeros_like(piece_out)
    piece_out[:, :width] = bias
    piece_out[:, value_at : value_at + value_width] = value_bias
    piece_copy = remote(piece_out, piece_in, piece_sem, before)
    piece_copy.start()

    length_copy.wait_recv()
    scatter = placement([length_in[c : c + 1, :1] for c in range(SLOTS)], rows, True)
    for g in range(KV_HEADS):
        side[g].wait_recv()
        back[g].start()
    piece_copy.wait_recv()
    bias_ref[...] = piece_in[:, :width]
    value_bias_ref[...] = piece_in[:, value_at : value_at + value_width]
    for g in range(KV_HEADS):
        home[g].wait_recv()
        back[g].wait_recv()
        slots = jnp.concatenate([home_in[g], side_in[g], back_in[g]], axis=0)
        arrived = dot(scatter, slots, ((1,), (0,))).astype(jnp.bfloat16)
        up_q_ref[:, g * QUERY_WIDTH : (g + 1) * QUERY_WIDTH] = arrived[:, :QUERY_WIDTH]
        at = slice(g * HEAD_DIM, (g + 1) * HEAD_DIM)
        up_k_ref[:, at] = arrived[:, QUERY_WIDTH : QUERY_WIDTH + HEAD_DIM]
        up_v_ref[:, at] = arrived[:, QUERY_WIDTH + HEAD_DIM :]
    for copy in home + side + lend + back + exchanges + [length_copy, piece_copy]:
        copy.wait_send()


def solution(mesh):
    dp, pipe = mesh.shape["dp"], mesh.shape["pipe"]
    columns = (HEADS + 2 * KV_HEADS) * HEAD_DIM
    steps = dp.bit_length() - 1

    def shards(queries, key_rows, value_rows, out_grad, log_norm, row_delta, cand_lengths):
        rows = queries.shape[1]
        width = (HEADS + KV_HEADS) * HEAD_DIM // dp
        value_width = KV_HEADS * HEAD_DIM // dp
        piece = up_to_lanes(width) + up_to_lanes(value_width)
        chunk = pltpu.VMEM((KV_HEADS, SLOT, CHUNK), jnp.bfloat16)
        dma = pltpu.SemaphoreType.DMA
        vmem = pl.BlockSpec(memory_space=pltpu.VMEM)
        kv = jax.ShapeDtypeStruct((rows, KV_HEADS * HEAD_DIM), jnp.bfloat16)
        outs = pl.pallas_call(
            functools.partial(kernel, dp, pipe),
            out_shape=(
                jax.ShapeDtypeStruct((rows, HEADS * HEAD_DIM), jnp.bfloat16),
                kv,
                kv,
                jax.ShapeDtypeStruct((1, width), jnp.float32),
                jax.ShapeDtypeStruct((1, value_width), jnp.float32),
            ),
            in_specs=[pl.BlockSpec(memory_space=pltpu.SMEM)] + [vmem] * 6,
            out_specs=[vmem] * 5,
            scratch_shapes=[chunk] * 8
            + [
                pltpu.VMEM((8, 128), jnp.int32),
                pltpu.VMEM((8, 128), jnp.int32),
                pltpu.VMEM((steps + 1, 1, columns), jnp.float32),
                pltpu.VMEM((steps, 1, columns), jnp.float32),
                pltpu.VMEM((1, piece), jnp.float32),
                pltpu.VMEM((1, piece), jnp.float32),
            ]
            + [dma((KV_HEADS, 2))] * 4
            + [dma((2,)), dma((steps, 2)), dma((2,))],
            compiler_params=pltpu.CompilerParams(
                collective_id=0, has_side_effects=True, vmem_limit_bytes=40 * 2**20
            ),
        )(
            cand_lengths, queries[0], key_rows[0], value_rows[0], out_grad[0],
            log_norm[0], row_delta[0],
        )
        return (outs[0][None], outs[1][None], outs[2][None], outs[3], outs[4])

    rows = P("pipe", "dp", None)
    heads = P("pipe", None, "dp")
    sums = P("pipe", "dp")
    return jax.shard_map(
        shards,
        mesh=mesh,
        in_specs=(rows, rows, rows, rows, heads, heads, rows),
        out_specs=(rows, rows, rows, sums, sums),
        check_vma=False,
    )
```

time: 106 us -> 53.2 us (0.50)
  Pallas kernels: 0 us -> 42.2 us
  waiting for transfers between devices: 32 us -> 0 us
  blocking collectives: 23.2 us -> 0 us
  matrix products: 16.1 us -> 0 us
  local copies, waits for them, and re-layouts: 23.3 us -> 10 us
  starting transfers between devices: 6.1 us -> 0 us
  other arithmetic: 2.22 us -> 0 us
  between operations: 2.06 us -> 0.66 us
    pallas_call x0 -> x1, Pallas kernels: none -> 42.2 us  [shards(): pl.pallas_call(functools.partial(kernel, dp, pipe), out_shape=(jax.ShapeD...]
    ppermute x3 -> x0, waiting for transfers between devices: 32 us -> none  [passed_along(): return lax.ppermute(value, axis, pairs)]
    unnamed x1 -> x0, blocking collectives: 23.2 us -> none
    dot_general x23 -> x0, matrix products: 16.1 us -> none  [the longest x4 4.55 us: one_group(): jnp.einsum('igd,jd->gij', grad_heads, value_group, preferred_element_type...]
    another operation x6 -> x0, local copies, waits for them, and re-layouts: 6.27 us -> none  [the longest x1 3.45 us: attend_backward(): grad_rows.reshape(row_count, KV_HEADS, per_group * HEAD_DIM)]
    ppermute x3 -> x0, starting transfers between devices: 6.1 us -> none  [passed_along(): return lax.ppermute(value, axis, pairs)]
    reshape x3 -> x0, local copies, waits for them, and re-layouts: 3.52 us -> none  [the longest x1 1.6 us: attend_backward(): jnp.moveaxis(grad_query, 0, 1).reshape(row_count, HEADS * HEAD_DIM)]
    dynamic_update_slice x4 -> x0, local copies, waits for them, and re-layouts: 3.01 us -> none  [attend_backward(): lax.map(one_group, (query_groups, key_groups, value_groups, grad_groups,...]
  transfers between devices with their start and end apart: 3 -> 0, of which waited for: 2 -> 0; matrix products, arithmetic and copies ran while one was open for 3% -> 0% of each run, Pallas kernels for 0% -> 0%
where the time goes in v1:
time: 53.2 us; the launch traced here: 52.9 us
  Pallas kernels  42.2 us (79%)
  local copies, waits for them, and re-layouts  10 us (19%)
  between operations  0.66 us (1%)
    pallas_call x1, Pallas kernels, shards(): pl.pallas_call(functools.partial(kernel, dp, pipe), out_shape=(jax.ShapeD...  42.2 us
    unnamed x19, local copies, waits for them, and re-layouts  10 us

profile of v1, /device:TPU:0, one launch (start us, length us, event | category | flops | bytes accessed | tf_op | source)
XLA Modules:
  0.0 52.9 jit_solution(8508001982574466459)
XLA Ops:
  0.6 0.0 copy-start
  0.6 1.3 %copy-done = bf16[1,240,2560]{2,1,0:T(8,128)(2,1)S(1)} copy-done((bf16[1,240,2560]{2,1,0:T(8,128)(2,1)S(1)}, bf16[1,240,2560]{2,1,0:T(8,128)(2,1)}, u32[]{:S(2)}) %copy-start) | copy-done | bytes 1228824
  1.9 0.0 copy-start.1
  1.9 1.3 %copy-done.1 = bf16[1,240,2560]{2,1,0:T(8,128)(2,1)S(1)} copy-done((bf16[1,240,2560]{2,1,0:T(8,128)(2,1)S(1)}, bf16[1,240,2560]{2,1,0:T(8,128)(2,1)}, u32[]{:S(2)}) %copy-start.1) | copy-done | bytes 1228824
  3.2 0.0 copy-start.2
  3.2 0.9 %copy-done.2 = bf16[1,240,512]{2,1,0:T(8,128)(2,1)S(1)} copy-done((bf16[1,240,512]{2,1,0:T(8,128)(2,1)S(1)}, bf16[1,240,512]{2,1,0:T(8,128)(2,1)}, u32[]{:S(2)}) %copy-start.2) | copy-done | bytes 245784
  4.2 0.0 copy-start.3
  4.2 0.9 %copy-done.3 = bf16[1,240,512]{2,1,0:T(8,128)(2,1)S(1)} copy-done((bf16[1,240,512]{2,1,0:T(8,128)(2,1)S(1)}, bf16[1,240,512]{2,1,0:T(8,128)(2,1)}, u32[]{:S(2)}) %copy-start.3) | copy-done | bytes 245784
  5.1 0.0 copy-start.4
  5.1 0.7 %copy-done.4 = bf16[1,20,240]{2,1,0:T(8,128)(2,1)S(1)} copy-done((bf16[1,20,240]{2,1,0:T(8,128)(2,1)S(1)}, bf16[1,20,240]{2,1,0:T(8,128)(2,1)}, u32[]{:S(2)}) %copy-start.4) | copy-done | bytes 9624
  5.8 0.0 copy-start.5
  5.8 0.7 %copy-done.5 = bf16[1,20,240]{2,1,0:T(8,128)(2,1)S(1)} copy-done((bf16[1,20,240]{2,1,0:T(8,128)(2,1)S(1)}, bf16[1,20,240]{2,1,0:T(8,128)(2,1)}, u32[]{:S(2)}) %copy-start.5) | copy-done | bytes 9624
  6.5 0.0 copy-start.6
  6.5 0.7 %copy-done.6 = s32[1,1,3]{2,1,0:T(1,128)S(1)} copy-done((s32[1,1,3]{2,1,0:T(1,128)S(1)}, s32[1,1,3]{2,1,0:T(1,128)}, u32[]{:S(2)}) %copy-start.6) | copy-done | bytes 36
  7.2 42.2 %shard_map.110 = (bf16[240,2560]{1,0:T(8,128)(2,1)S(1)}, bf16[240,512]{1,0:T(8,128)(2,1)S(1)}, bf16[240,512]{1,0:T(8,128)(2,1)S(1)}, f32[1,384]{1,0:T(1,128)S(1)}, f32[1,64]{1,0:T(1,128)S(1)}) custom-call(s32[1,1,3]{2,1,0:T(1,128)S(1)} %copy-done.6, bf16[240,2560]{1,0:T(8,128)(2,1)S(1)} %bitcast.9, bf16[240,512]{1,0:T(8,128)(2,1)S(1)} %bitcast.12, ...), custom_call_target="tpu_custom_call" | custom-call | tf_op jit(solution)/shard_map/pallas_call | solution.py:210
  49.4 1.0 %copy.17 = bf16[1,240,2560]{2,1,0:T(8,128)(2,1)} copy(bf16[1,240,2560]{2,1,0:T(8,128)(2,1)S(1)} %bitcast.11) | data formatting | bytes 2457600
  50.4 0.7 %copy.18 = bf16[1,240,512]{2,1,0:T(8,128)(2,1)} copy(bf16[1,240,512]{2,1,0:T(8,128)(2,1)S(1)} %bitcast.15) | data formatting | bytes 491520
  51.1 0.7 %copy.19 = bf16[1,240,512]{2,1,0:T(8,128)(2,1)} copy(bf16[1,240,512]{2,1,0:T(8,128)(2,1)S(1)} %bitcast.14) | data formatting | bytes 491520
  51.8 0.6 %copy.20 = f32[1,384]{1,0:T(1,128)} copy(f32[1,384]{1,0:T(1,128)S(1)} %get-tuple-element.23) | data formatting | bytes 3072
  52.4 0.5 copy.21
Async XLA Ops:
  0.6 1.3 %copy-start = (bf16[1,240,2560]{2,1,0:T(8,128)(2,1)S(1)}, bf16[1,240,2560]{2,1,0:T(8,128)(2,1)}, u32[]{:S(2)}) copy-start(bf16[1,240,2560]{2,1,0:T(8,128)(2,1)} %param.7) | copy-start | bytes 3686404
  1.9 1.3 %copy-start.1 = (bf16[1,240,2560]{2,1,0:T(8,128)(2,1)S(1)}, bf16[1,240,2560]{2,1,0:T(8,128)(2,1)}, u32[]{:S(2)}) copy-start(bf16[1,240,2560]{2,1,0:T(8,128)(2,1)} %param.10) | copy-start | bytes 3686404
  3.2 0.9 %copy-start.2 = (bf16[1,240,512]{2,1,0:T(8,128)(2,1)S(1)}, bf16[1,240,512]{2,1,0:T(8,128)(2,1)}, u32[]{:S(2)}) copy-start(bf16[1,240,512]{2,1,0:T(8,128)(2,1)} %param.8) | copy-start | bytes 737284
  4.2 0.9 %copy-start.3 = (bf16[1,240,512]{2,1,0:T(8,128)(2,1)S(1)}, bf16[1,240,512]{2,1,0:T(8,128)(2,1)}, u32[]{:S(2)}) copy-start(bf16[1,240,512]{2,1,0:T(8,128)(2,1)} %param.9) | copy-start | bytes 737284
  5.1 0.7 %copy-start.4 = (bf16[1,20,240]{2,1,0:T(8,128)(2,1)S(1)}, bf16[1,20,240]{2,1,0:T(8,128)(2,1)}, u32[]{:S(2)}) copy-start(bf16[1,20,240]{2,1,0:T(8,128)(2,1)} %param.11) | copy-start | bytes 28804
  5.8 0.7 %copy-start.5 = (bf16[1,20,240]{2,1,0:T(8,128)(2,1)S(1)}, bf16[1,20,240]{2,1,0:T(8,128)(2,1)}, u32[]{:S(2)}) copy-start(bf16[1,20,240]{2,1,0:T(8,128)(2,1)} %param.12) | copy-start | bytes 28804
  6.5 0.7 %copy-start.6 = (s32[1,1,3]{2,1,0:T(1,128)S(1)}, s32[1,1,3]{2,1,0:T(1,128)}, u32[]{:S(2)}) copy-start(s32[1,1,3]{2,1,0:T(1,128)} %lengths_ref.1) | copy-start | bytes 40

commit v2 on v1

--- a/solution.py
+++ b/solution.py
@@ -43,12 +43,24 @@
 
 
 def kernel(
-    dp, pipe, lengths_ref, q_ref, k_ref, v_ref, g_ref, norm_ref, delta_ref,
+    dp, pipe, lengths_hbm, q_hbm, k_hbm, v_hbm, g_hbm, norm_hbm, delta_hbm,
     up_q_ref, up_k_ref, up_v_ref, bias_ref, value_bias_ref,
+    lengths_ref, q_ref, k_ref, v_ref, g_ref, norm_ref, delta_ref, fetch_sem,
     home_out, side_out, own_second, pair_out, home_in, side_in, pair_in, back_in,
     length_out, length_in, sums, sums_in, piece_out, piece_in,
     home_sem, side_sem, pair_sem, back_sem, length_sem, sums_sem, piece_sem,
 ):
+    fetched = [(lengths_hbm, lengths_ref), (norm_hbm, norm_ref), (delta_hbm, delta_ref)]
+    fetched += [(k_hbm, k_ref), (v_hbm, v_ref)]
+    for g in range(KV_HEADS):
+        at = pl.ds(g * QUERY_WIDTH, QUERY_WIDTH)
+        fetched += [(q_hbm.at[:, at], q_ref.at[:, at]), (g_hbm.at[:, at], g_ref.at[:, at])]
+    fetches = [
+        pltpu.make_async_copy(src, dst, fetch_sem.at[i]) for i, (src, dst) in enumerate(fetched)
+    ]
+    for fetch in fetches:
+        fetch.start()
+
     me, stage = lax.axis_index("dp"), lax.axis_index("pipe")
     before = {"dp": me, "pipe": (stage + pipe - 1) % pipe}
     after = {"dp": me, "pipe": (stage + 1) % pipe}
@@ -70,6 +82,8 @@
             device_id=device, device_id_type=MESH,
         )
 
+    for fetch in fetches[:3]:
+        fetch.wait()
     lengths = [lengths_ref[0, 0, c] for c in range(SLOTS)]
     line = lax.broadcasted_iota(jnp.int32, (8, 128), 0)
     length_out[...] = jnp.where(
@@ -93,12 +107,18 @@
     def taken(ref, begin, width):
         return dot(gather, ref[:, begin : begin + width], ((1,), (0,))).astype(jnp.bfloat16)
 
+    early = KV_HEADS // 2
+
     def send_side(g):
         lend[g].wait_recv()
         side_out[g] = own_second[g] + pair_in[g]
         side[g].start()
 
+    for fetch in fetches[3:5]:
+        fetch.wait()
     for g in range(KV_HEADS):
+        for fetch in fetches[5 + 2 * g : 7 + 2 * g]:
+            fetch.wait()
         queries = taken(q_ref, g * QUERY_WIDTH, QUERY_WIDTH)
         grads = taken(g_ref, g * QUERY_WIDTH, QUERY_WIDTH)
         keys = taken(k_ref, g * HEAD_DIM, HEAD_DIM)
@@ -133,7 +153,7 @@
             held[g, :, QUERY_WIDTH + HEAD_DIM :] = grad_v
             if c == 2:
                 lend[g].start()
-            if c == 0:
+            if c == 0 and g < early:
                 home[g].start()
         total = dot(
             ones,
@@ -147,15 +167,24 @@
             sums[0, :, begin : begin + HEAD_DIM] = total[:, part : part + HEAD_DIM]
         if g > 0:
             send_side(g - 1)
+    exchanges = [
+        remote(sums.at[i], sums_in.at[i], sums_sem.at[i], across(step))
+        for i, step in enumerate(steps)
+    ]
+    exchanges[0].start()
     send_side(KV_HEADS - 1)
-
-    exchanges = []
-    for i, step in enumerate(steps):
-        exchange = remote(sums.at[i], sums_in.at[i], sums_sem.at[i], across(step))
-        exchange.start()
-        exchange.wait_recv()
-        sums[i + 1] = sums[i] + sums_in[i]
-        exchanges.append(exchange)
+    home[early].start()
+    for i in range(max(KV_HEADS, len(steps))):
+        if i < KV_HEADS:
+            side[i].wait_recv()
+            back[i].start()
+        if early + 1 + i < KV_HEADS:
+            home[early + 1 + i].start()
+        if i < len(steps):
+            exchanges[i].wait_recv()
+            sums[i + 1] = sums[i] + sums_in[i]
+            if i + 1 < len(steps):
+                exchanges[i + 1].start()
     total = sums[len(steps)]
     width, value_width = bias_ref.shape[1], value_bias_ref.shape[1]
     value_at = up_to_lanes(width)
@@ -175,12 +204,6 @@
     length_copy.wait_recv()
     scatter = placement([length_in[c : c + 1, :1] for c in range(SLOTS)], rows, True)
     for g in range(KV_HEADS):
-        side[g].wait_recv()
-        back[g].start()
-    piece_copy.wait_recv()
-    bias_ref[...] = piece_in[:, :width]
-    value_bias_ref[...] = piece_in[:, value_at : value_at + value_width]
-    for g in range(KV_HEADS):
         home[g].wait_recv()
         back[g].wait_recv()
         slots = jnp.concatenate([home_in[g], side_in[g], back_in[g]], axis=0)
@@ -189,8 +212,23 @@
         at = slice(g * HEAD_DIM, (g + 1) * HEAD_DIM)
         up_k_ref[:, at] = arrived[:, QUERY_WIDTH : QUERY_WIDTH + HEAD_DIM]
         up_v_ref[:, at] = arrived[:, QUERY_WIDTH + HEAD_DIM :]
+    piece_copy.wait_recv()
+    bias_ref[...] = piece_in[:, :width]
+    value_bias_ref[...] = piece_in[:, value_at : value_at + value_width]
     for copy in home + side + lend + back + exchanges + [length_copy, piece_copy]:
         copy.wait_send()
+
+
+def written(*refs):
+    count = len(refs) // 2
+    sems = refs[-1]
+    copies = [
+        pltpu.make_async_copy(refs[i], refs[count + i], sems.at[i]) for i in range(count)
+    ]
+    for copy in copies:
+        copy.start()
+    for copy in copies:
+        copy.wait()
 
 
 def solution(mesh):
@@ -207,18 +245,27 @@
         dma = pltpu.SemaphoreType.DMA
         vmem = pl.BlockSpec(memory_space=pltpu.VMEM)
         kv = jax.ShapeDtypeStruct((rows, KV_HEADS * HEAD_DIM), jnp.bfloat16)
+        hbm = pl.BlockSpec(memory_space=pltpu.HBM)
+        shapes = (
+            jax.ShapeDtypeStruct((rows, HEADS * HEAD_DIM), jnp.bfloat16),
+            kv,
+            kv,
+            jax.ShapeDtypeStruct((1, width), jnp.float32),
+            jax.ShapeDtypeStruct((1, value_width), jnp.float32),
+        )
+        operands = (
+            cand_lengths, queries[0], key_rows[0], value_rows[0], out_grad[0],
+            log_norm[0], row_delta[0],
+        )
         outs = pl.pallas_call(
             functools.partial(kernel, dp, pipe),
-            out_shape=(
-                jax.ShapeDtypeStruct((rows, HEADS * HEAD_DIM), jnp.bfloat16),
-                kv,
-                kv,
-                jax.ShapeDtypeStruct((1, width), jnp.float32),
-                jax.ShapeDtypeStruct((1, value_width), jnp.float32),
-            ),
-            in_specs=[pl.BlockSpec(memory_space=pltpu.SMEM)] + [vmem] * 6,
+            out_shape=shapes,
+            in_specs=[hbm] * len(operands),
             out_specs=[vmem] * 5,
-            scratch_shapes=[chunk] * 8
+            scratch_shapes=[pltpu.SMEM(cand_lengths.shape, jnp.int32)]
+            + [pltpu.VMEM(x.shape, x.dtype) for x in operands[1:]]
+            + [dma((5 + 2 * KV_HEADS,))]
+            + [chunk] * 8
             + [
                 pltpu.VMEM((8, 128), jnp.int32),
                 pltpu.VMEM((8, 128), jnp.int32),
@@ -230,12 +277,17 @@
             + [dma((KV_HEADS, 2))] * 4
             + [dma((2,)), dma((steps, 2)), dma((2,))],
             compiler_params=pltpu.CompilerParams(
-                collective_id=0, has_side_effects=True, vmem_limit_bytes=40 * 2**20
+                collective_id=0, has_side_effects=True, vmem_limit_bytes=56 * 2**20
             ),
-        )(
-            cand_lengths, queries[0], key_rows[0], value_rows[0], out_grad[0],
-            log_norm[0], row_delta[0],
-        )
+        )(*operands)
+        outs = pl.pallas_call(
+            written,
+            out_shape=shapes,
+            in_specs=[hbm] * 5,
+            out_specs=[hbm] * 5,
+            scratch_shapes=[dma((5,))],
+            compiler_params=pltpu.CompilerParams(vmem_limit_bytes=56 * 2**20),
+        )(*outs)
         return (outs[0][None], outs[1][None], outs[2][None], outs[3], outs[4])
 
     rows = P("pipe", "dp", None)

time: 53.2 us -> 90.1 us (1.69)
  Pallas kernels: 42.2 us -> 89.3 us
  local copies, waits for them, and re-layouts: 10 us -> 0 us
    pallas_call x1 -> x2, Pallas kernels: 42.2 us -> 89.3 us  [the longest x1 53.3 us: shards(): pl.pallas_call(written, out_shape=shapes, in_specs=[hbm] * 5, out_specs=[...]
    unnamed x19 -> x0, local copies, waits for them, and re-layouts: 10 us -> none
where the time goes in v2:
time: 90.1 us; the launch traced here: 90 us
  Pallas kernels  89.3 us (99%)
    pallas_call x1, Pallas kernels, shards(): pl.pallas_call(written, out_shape=shapes, in_specs=[hbm] * 5, out_specs=[...  53.3 us
    pallas_call x1, Pallas kernels, shards(): pl.pallas_call(functools.partial(kernel, dp, pipe), out_shape=shapes, in_...  36 us

profile of v2, /device:TPU:0, one launch (start us, length us, event | category | flops | bytes accessed | tf_op | source)
XLA Modules:
  0.0 90.0 jit_solution(16587597093492151889)
XLA Ops:
  0.6 36.0 %shard_map.110 = (bf16[240,2560]{1,0:T(8,128)(2,1)}, bf16[240,512]{1,0:T(8,128)(2,1)}, bf16[240,512]{1,0:T(8,128)(2,1)}, f32[1,384]{1,0:T(1,128)}, f32[1,64]{1,0:T(1,128)}) custom-call(s32[1,1,3]{2,1,0:T(1,128)} %lengths_hbm.1, bf16[240,2560]{1,0:T(8,128)(2,1)} %bitcast.9, bf16[240,512]{1,0:T(8,128)(2,1)} %bitcast.11, bf16[240,512]{1,0:T(8,128)(2,1)} %bitcast.12, ...), custom_call_target="tpu_custom_call" | custom-call | tf_op jit(solution)/shard_map/pallas_call | solution.py:260
  36.7 53.3 %shard_map.111 = (bf16[240,2560]{1,0:T(8,128)(2,1)}, bf16[240,512]{1,0:T(8,128)(2,1)}, bf16[240,512]{1,0:T(8,128)(2,1)}, f32[1,384]{1,0:T(1,128)}, f32[1,64]{1,0:T(1,128)}) custom-call(bf16[240,2560]{1,0:T(8,128)(2,1)} %get-tuple-element.15.refs_0_, bf16[240,512]{1,0:T(8,128)(2,1)} %get-tuple-element.16.refs_1_, bf16[240,512]{1,0:T(8,128)(2,1)} %get-tuple-element.17.refs_2_, ...), custom_call_target="tpu_custom_call" | custom-call | tf_op jit(solution)/shard_map/pallas_call | solution.py:283

commit v3 on v2

--- a/solution.py
+++ b/solution.py
@@ -277,16 +277,16 @@
             + [dma((KV_HEADS, 2))] * 4
             + [dma((2,)), dma((steps, 2)), dma((2,))],
             compiler_params=pltpu.CompilerParams(
-                collective_id=0, has_side_effects=True, vmem_limit_bytes=56 * 2**20
+                collective_id=0, has_side_effects=True, vmem_limit_bytes=40 * 2**20
             ),
-        )(*operands)
+        )(*[pltpu.with_memory_space_constraint(x, pltpu.HBM) for x in operands])
         outs = pl.pallas_call(
             written,
             out_shape=shapes,
-            in_specs=[hbm] * 5,
+            in_specs=[vmem] * 5,
             out_specs=[hbm] * 5,
             scratch_shapes=[dma((5,))],
-            compiler_params=pltpu.CompilerParams(vmem_limit_bytes=56 * 2**20),
+            compiler_params=pltpu.CompilerParams(vmem_limit_bytes=16 * 2**20),
         )(*outs)
         return (outs[0][None], outs[1][None], outs[2][None], outs[3], outs[4])
 

time: 90.1 us -> 36.8 us (0.41)
  Pallas kernels: 89.3 us -> 36.1 us
    pallas_call x1, Pallas kernels: 53.3 us -> 1.23 us  [shards(): pl.pallas_call(written, out_shape=shapes, in_specs=[vmem] * 5, out_specs=...]
    pallas_call x1, Pallas kernels: 36 us -> 34.8 us  [shards(): pl.pallas_call(functools.partial(kernel, dp, pipe), out_shape=shapes, in_...]
where the time goes in v3:
time: 36.8 us; the launch traced here: 36.7 us
  Pallas kernels  36.1 us (98%)
  between operations  0.64 us (2%)
    pallas_call x1, Pallas kernels, shards(): pl.pallas_call(functools.partial(kernel, dp, pipe), out_shape=shapes, in_...  34.8 us
    pallas_call x1, Pallas kernels, shards(): pl.pallas_call(written, out_shape=shapes, in_specs=[vmem] * 5, out_specs=...  1.23 us

profile of v3, /device:TPU:0, one launch (start us, length us, event | category | flops | bytes accessed | tf_op | source)
XLA Modules:
  0.0 36.7 jit_solution(8595240477192868057)
XLA Ops:
  0.6 34.8 %shard_map.110 = (bf16[240,2560]{1,0:T(8,128)(2,1)S(1)}, bf16[240,512]{1,0:T(8,128)(2,1)S(1)}, bf16[240,512]{1,0:T(8,128)(2,1)S(1)}, f32[1,384]{1,0:T(1,128)S(1)}, f32[1,64]{1,0:T(1,128)S(1)}) custom-call(s32[1,1,3]{2,1,0:T(1,128)} %lengths_hbm.1, bf16[240,2560]{1,0:T(8,128)(2,1)} %bitcast.9, bf16[240,512]{1,0:T(8,128)(2,1)} %bitcast.11, ...), custom_call_target="tpu_custom_call" | custom-call | tf_op jit(solution)/shard_map/pallas_call | solution.py:260
  35.5 1.2 %shard_map.111 = (bf16[240,2560]{1,0:T(8,128)(2,1)}, bf16[240,512]{1,0:T(8,128)(2,1)}, bf16[240,512]{1,0:T(8,128)(2,1)}, f32[1,384]{1,0:T(1,128)}, f32[1,64]{1,0:T(1,128)}) custom-call(bf16[240,2560]{1,0:T(8,128)(2,1)S(1)} %get-tuple-element.15.refs_0_, bf16[240,512]{1,0:T(8,128)(2,1)S(1)} %get-tuple-element.16.refs_1_, ...), custom_call_target="tpu_custom_call" | custom-call | tf_op jit(solution)/shard_map/pallas_call | solution.py:283

commit v4 on v3

--- a/solution.py
+++ b/solution.py
@@ -123,7 +123,7 @@
         grads = taken(g_ref, g * QUERY_WIDTH, QUERY_WIDTH)
         keys = taken(k_ref, g * HEAD_DIM, HEAD_DIM)
         values = taken(v_ref, g * HEAD_DIM, HEAD_DIM)
-        for c in (2, 0, 1):
+        for c in (0, 2, 1) if g == 0 else (2, 0, 1):
             at = slice(c * SLOT, (c + 1) * SLOT)
             heads = range(PER_GROUP)
 

time: 36.8 us -> 37.2 us (1.011)
  no operation moved by 1% of the time
where the time goes in v4:
time: 37.2 us; the launch traced here: 37 us
  Pallas kernels  36.4 us (98%)
  between operations  0.64 us (2%)
    pallas_call x1, Pallas kernels, shards(): pl.pallas_call(functools.partial(kernel, dp, pipe), out_shape=shapes, in_...  35.2 us
    pallas_call x1, Pallas kernels, shards(): pl.pallas_call(written, out_shape=shapes, in_specs=[vmem] * 5, out_specs=...  1.23 us

profile of v4, /device:TPU:0, one launch (start us, length us, event | category | flops | bytes accessed | tf_op | source)
XLA Modules:
  0.0 37.0 jit_solution(13136582715314378794)
XLA Ops:
  0.6 35.2 %shard_map.110 = (bf16[240,2560]{1,0:T(8,128)(2,1)S(1)}, bf16[240,512]{1,0:T(8,128)(2,1)S(1)}, bf16[240,512]{1,0:T(8,128)(2,1)S(1)}, f32[1,384]{1,0:T(1,128)S(1)}, f32[1,64]{1,0:T(1,128)S(1)}) custom-call(s32[1,1,3]{2,1,0:T(1,128)} %lengths_hbm.1, bf16[240,2560]{1,0:T(8,128)(2,1)} %bitcast.9, bf16[240,512]{1,0:T(8,128)(2,1)} %bitcast.11, ...), custom_call_target="tpu_custom_call" | custom-call | tf_op jit(solution)/shard_map/pallas_call | solution.py:260
  35.8 1.2 %shard_map.111 = (bf16[240,2560]{1,0:T(8,128)(2,1)}, bf16[240,512]{1,0:T(8,128)(2,1)}, bf16[240,512]{1,0:T(8,128)(2,1)}, f32[1,384]{1,0:T(1,128)}, f32[1,64]{1,0:T(1,128)}) custom-call(bf16[240,2560]{1,0:T(8,128)(2,1)S(1)} %get-tuple-element.15.refs_0_, bf16[240,512]{1,0:T(8,128)(2,1)S(1)} %get-tuple-element.16.refs_1_, ...), custom_call_target="tpu_custom_call" | custom-call | tf_op jit(solution)/shard_map/pallas_call | solution.py:283
